TPU v7x, 32 devices: a whole 2x2x4 slice. The times are simulated.
32 devices in a mesh: seq: 4 (over x, core), row: 4 (over z), col: 2 (over y).
Axes of the slice: x: 2, y: 2, z: 4, core: 2. Of those that a mesh axis runs over, the one named last changes fastest.
Arguments:
- homolog_activations: bfloat16 [32, 64, 64], P(('seq', 'col'), 'row'), may hold values from -6 to 6
- alignment_token_ids: int32 [32, 64], P(('seq', 'col'), 'row'), may hold values from 0 to 79
- symbol_lookup_matrix: bfloat16 [80, 64], replicated, may hold values from -6 to 6
- homolog_rescale_vector: float32 [64], replicated, may hold values from 0.1 to 1.9
- first_operand_projection: bfloat16 [64, 32], replicated, may hold values from -0.75 to 0.75
- second_operand_projection: bfloat16 [64, 32], replicated, may hold values from -0.75 to 0.75
- outer_output_weight: bfloat16 [1024, 128], replicated, may hold values from -0.75 to 0.75
- outer_bias: float32 [128], replicated, may hold values from -3 to 3
- pair: bfloat16 [64, 64, 128], P('row', ('seq', 'col')), may hold values from -6 to 6
- pair_norm_gain: float32 [128], replicated, may hold values from 0.1 to 1.9
- pair_query_weight: bfloat16 [128, 128], replicated, as said below
- pair_key_weight: bfloat16 [128, 128], replicated, as said below
- pair_value_weight: bfloat16 [128, 128], replicated, may hold values from -0.5 to 0.5
- pair_gate_weight: bfloat16 [128, 128], replicated, may hold values from -0.5 to 0.5
- pair_output_weight: bfloat16 [128, 128], replicated, may hold values from -0.5 to 0.5
- nodes: bfloat16 [64, 64], P(('seq', 'col')), may hold values from -6 to 6
- coords: float32 [3, 64], P(None, ('seq', 'col')), may hold values from -18 to 18
- neighbour_index: int32 [64, 64], P(('seq', 'col')), may hold values from 0 to 63
- neighbour_count: int32 [64], P(('seq', 'col')), may hold values from 1 to 64, 2560 in all
- node_norm_gain: float32 [64], replicated, may hold values from 0.1 to 1.9
- node_query_weight: bfloat16 [64, 64], replicated, as said below
- node_key_weight: bfloat16 [64, 64], replicated, as said below
- node_value_weight: bfloat16 [64, 64], replicated, may hold values from -0.75 to 0.75
- node_output_weight: bfloat16 [64, 64], replicated, may hold values from -0.75 to 0.75
- distance_penalty: float32 [4], replicated, may hold values from 0.02 to 0.5
- coordinate_step: float32 [4], replicated, may hold values from -0.5 to 0.5
Outputs:
- pair_out: bfloat16 [64, 64, 128], P('row', ('seq', 'col'))
- nodes_out: bfloat16 [64, 64], P(('seq', 'col'))
- coords_out: float32 [3, 64], P(None, ('seq', 'col'))
Inputs may be any that keep to these rules, and one draw needn't show every extreme that they name: `neighbour_index`: indices of residues; only the first neighbour_count[i] entries of row i are used. `pair_query_weight`: a projection matrix. `pair_key_weight`: a projection matrix. `node_query_weight`: a projection matrix. `node_key_weight`: a projection matrix.
All inputs are finite; a program needn't handle non-finite values. No bound on the sum of `neighbour_count` on one device may be relied on, other than what follows from the above.
Results may differ from a plain program's by a relative error of at most 0.02.
Values may be sent and summed in bfloat16 or wider, within the bound.
A program may use at most 64 MiB of HBM per device.

v0:
```python
from functools import partial

import jax
import jax.numpy as jnp
from jax import lax
from jax.sharding import PartitionSpec as P

PAIR_HEADS = 4
NODE_HEADS = 4


def spread(value, axis, source):
    kept = jnp.where(lax.axis_index(axis) == source, value, 0).astype(value.dtype)
    return lax.psum(kept, axis)


def layer_normalize(values_in, gain_vec):
    average = jnp.mean(values_in, -1, keepdims=True)
    centred = values_in - average
    variance = jnp.mean(centred * centred, -1, keepdims=True)
    return centred * lax.rsqrt(variance + 1e-05) * gain_vec


def attend_row(row_in, gain_vec, w_joined, w_out):
    length, channels = row_in.shape
    head_dim = channels // PAIR_HEADS
    normed = layer_normalize(row_in.astype(jnp.float32), gain_vec).astype(jnp.bfloat16)
    projected = jnp.dot(normed, w_joined, preferred_element_type=jnp.float32)
    queries = projected[:, :channels].astype(jnp.bfloat16).reshape(length, PAIR_HEADS, head_dim)
    keys_row = (
        projected[:, channels : 2 * channels]
        .astype(jnp.bfloat16)
        .reshape(length, PAIR_HEADS, head_dim)
    )
    values_row = (
        projected[:, 2 * channels : 3 * channels]
        .astype(jnp.bfloat16)
        .reshape(length, PAIR_HEADS, head_dim)
    )
    gates = projected[:, 3 * channels :]
    scores = jnp.einsum(
        "qhd,khd->hqk", queries, keys_row, preferred_element_type=jnp.float32
    ) * head_dim ** (-0.5)
    weights = jax.nn.softmax(scores, axis=-1).astype(jnp.bfloat16)
    attended = jnp.einsum(
        "hqk,khd->qhd", weights, values_row, preferred_element_type=jnp.float32
    ).reshape(length, channels)
    attended = (attended * jax.nn.sigmoid(gates)).astype(jnp.bfloat16)
    update = jnp.dot(attended, w_out, preferred_element_type=jnp.float32)
    return (row_in.astype(jnp.float32) + update).astype(jnp.bfloat16)


def on_device(
    homolog_activations,
    alignment_token_ids,
    symbol_lookup_matrix,
    homolog_rescale_vector,
    first_operand_projection,
    second_operand_projection,
    outer_output_weight,
    outer_bias,
    pair,
    pair_norm_gain,
    pair_query_weight,
    pair_key_weight,
    pair_value_weight,
    pair_gate_weight,
    pair_output_weight,
    nodes,
    coords,
    neighbour_index,
    neighbour_count,
    node_norm_gain,
    node_query_weight,
    node_key_weight,
    node_value_weight,
    node_output_weight,
    distance_penalty,
    coordinate_step,
):
    groups = lax.axis_size(("seq", "col"))
    rows_i, cols_j, channels = pair.shape
    sequences_local = homolog_activations.shape[0]
    total_seqs = sequences_local * groups
    outer_width = first_operand_projection.shape[1]
    token_kinds = symbol_lookup_matrix.shape[0]
    token_indicator = (
        alignment_token_ids[:, :, None] == jnp.arange(token_kinds, dtype=jnp.int32)
    ).astype(jnp.bfloat16)
    token_embedded = jnp.einsum(
        "sla,ac->slc", token_indicator, symbol_lookup_matrix, preferred_element_type=jnp.float32
    )
    alignment_normed = layer_normalize(
        homolog_activations.astype(jnp.float32) + token_embedded, homolog_rescale_vector
    )
    left_factor = (
        jnp.dot(alignment_normed, first_operand_projection, preferred_element_type=jnp.float32)
        .astype(jnp.bfloat16)
        .reshape(sequences_local, rows_i * outer_width)
    )
    right_factor = (
        jnp.dot(alignment_normed, second_operand_projection, preferred_element_type=jnp.float32)
        .astype(jnp.bfloat16)
        .reshape(sequences_local, rows_i * outer_width)
    )
    contract = (((0,), (0,)), ((), ()))
    left_all, right_all = (
        lax.all_gather(left_factor, ("seq", "col"), axis=0, tiled=True),
        lax.all_gather(right_factor, ("seq", "col"), axis=0, tiled=True),
    )
    position = lax.axis_index(("seq", "col"))
    root_row = position * cols_j // rows_i
    first_col = (position * cols_j - root_row * rows_i) * outer_width
    segment = lax.dynamic_slice_in_dim(right_all, first_col, cols_j * outer_width, 1)
    right_cols = spread(segment, "row", root_row)
    summed = lax.dot_general(left_all, right_cols, contract, preferred_element_type=jnp.float32)
    outer = (summed / total_seqs).reshape(rows_i, outer_width, cols_j, outer_width)
    outer = (
        outer.transpose(0, 2, 1, 3)
        .reshape(rows_i, cols_j, outer_width * outer_width)
        .astype(jnp.bfloat16)
    )
    pair_mid = (
        pair.astype(jnp.float32)
        + jnp.dot(outer, outer_output_weight, preferred_element_type=jnp.float32)
        + outer_bias
    ).astype(jnp.bfloat16)
    w_joined = jnp.concatenate(
        [pair_query_weight, pair_key_weight, pair_value_weight, pair_gate_weight], 1
    )
    sectioned = pair_mid.reshape(groups, rows_i // groups, cols_j, channels)
    results = lax.map(
        partial(attend_row, gain_vec=pair_norm_gain, w_joined=w_joined, w_out=pair_output_weight),
        lax.all_to_all(sectioned, ("seq", "col"), split_axis=0, concat_axis=2, tiled=True)[0],
    )
    row_major = results[None]
    returned = lax.all_to_all(row_major, ("seq", "col"), split_axis=2, concat_axis=0, tiled=True)
    pair_out = returned.reshape(rows_i, cols_j, channels)
    local_nodes, node_width = nodes.shape
    node_dim = node_width // NODE_HEADS
    slots = neighbour_index.shape[1]
    node_norm = layer_normalize(nodes.astype(jnp.float32), node_norm_gain).astype(jnp.bfloat16)
    node_proj = jnp.dot(
        node_norm,
        jnp.concatenate([node_query_weight, node_key_weight, node_value_weight], 1),
        preferred_element_type=jnp.float32,
    )
    node_query = (
        node_proj[:, :node_width].astype(jnp.bfloat16).reshape(local_nodes, NODE_HEADS, node_dim)
    )
    key_value = node_proj[:, node_width:].astype(jnp.bfloat16)
    table_wide, where_all = (
        lax.all_gather(key_value.astype(jnp.float32), ("seq", "col"), axis=0, tiled=True),
        lax.all_gather(coords, ("seq", "col"), axis=1, tiled=True),
    )
    node_table = table_wide.astype(jnp.bfloat16)
    neighbour_rows = node_table[neighbour_index]
    near_key = neighbour_rows[:, :, :node_width].reshape(local_nodes, slots, NODE_HEADS, node_dim)
    near_value = neighbour_rows[:, :, node_width:].reshape(local_nodes, slots, NODE_HEADS, node_dim)
    offsets = where_all[:, neighbour_index] - coords[:, :, None]
    dist2 = jnp.sum(offsets * offsets, 0)
    logits = jnp.einsum(
        "ihd,ikhd->ihk", node_query, near_key, preferred_element_type=jnp.float32
    ) * node_dim ** (-0.5)
    logits = logits - distance_penalty[None, :, None] * dist2[:, None, :]
    is_valid = jnp.arange(slots, dtype=jnp.int32)[None, :] < neighbour_count[:, None]
    logits = jnp.where(is_valid[:, None, :], logits, -1e30)
    node_weight = jax.nn.softmax(logits, axis=-1)
    node_weight = jnp.where(is_valid[:, None, :], node_weight, 0.0)
    node_mix = jnp.einsum(
        "ihk,ikhd->ihd",
        node_weight.astype(jnp.bfloat16),
        near_value,
        preferred_element_type=jnp.float32,
    )
    node_mix = node_mix.reshape(local_nodes, node_width).astype(jnp.bfloat16)
    nodes_out = (
        nodes.astype(jnp.float32)
        + jnp.dot(node_mix, node_output_weight, preferred_element_type=jnp.float32)
    ).astype(jnp.bfloat16)
    coord_pull = jnp.sum(node_weight * coordinate_step[None, :, None], 1)
    coords_out = coords + jnp.sum(offsets * coord_pull[None], -1)
    return (pair_out, nodes_out, coords_out)


def solution(mesh):
    placed = (
        P(("seq", "col"), "row", None),
        P(("seq", "col"), "row"),
        P(),
        P(),
        P(),
        P(),
        P(),
        P(),
        P("row", ("seq", "col"), None),
        P(),
        P(),
        P(),
        P(),
        P(),
        P(),
        P(("seq", "col"), None),
        P(None, ("seq", "col")),
        P(("seq", "col"), None),
        P(("seq", "col")),
        P(),
        P(),
        P(),
        P(),
        P(),
        P(),
        P(),
    )
    return jax.shard_map(
        on_device,
        mesh=mesh,
        in_specs=placed,
        out_specs=(
            P("row", ("seq", "col"), None),
            P(("seq", "col"), None),
            P(None, ("seq", "col")),
        ),
        check_vma=False,
    )
```

profile of v0, /device:TPU:0, one launch (start us, length us, event | category | flops | bytes accessed | tf_op | source)
XLA Modules:
  0.0 110.4 jit_solution(7726163937578267045)
XLA Ops:
  0.7 0.7 copy-done.14
  1.9 0.5 copy-done.21
  2.8 14.4 %all-gather.1 = bf16[8,4,512]{2,1,0:T(4,128)(2,1)S(1)} all-gather(bf16[1,4,512]{2,1,0:T(4,128)(2,1)S(1)} %reshape.144), channel_id=1, replica_groups=mesh['seq'=4,'row'=4,'col'=2] {'seq','col'}, dimensions={0}, use_global_device_ids=true | all-gather | bytes 36864 | tf_op jit(solution)/shard_map/all_gather | solution.py:109
  17.3 19.0 %psum.7 = bf16[32,256]{1,0:T(8,128)(2,1)S(1)} all-reduce(bf16[32,256]{1,0:T(8,128)(2,1)S(1)} %dynamic-slice_select_fusion), channel_id=1, replica_groups=mesh['seq'=4,'row'=4,'col'=2] {'row'}, use_global_device_ids=true, to_apply=%region_2.3 | all-reduce | flops 8192 | bytes 32768 | tf_op jit(solution)/shard_map/psum | solution.py:14
  36.6 12.5 %all-gather = bf16[8,4,512]{2,1,0:T(4,128)(2,1)S(1)} all-gather(bf16[1,4,512]{2,1,0:T(4,128)(2,1)S(1)} %reshape.142), channel_id=1, replica_groups=mesh['seq'=4,'row'=4,'col'=2] {'seq','col'}, dimensions={0}, use_global_device_ids=true | all-gather | bytes 36864 | tf_op jit(solution)/shard_map/all_gather | solution.py:108
  50.1 1.1 convert_element_type.86
  51.2 0.8 fusion.34
  52.1 3.9 %all-to-all-start = ((bf16[8,2,8,128]{3,2,1,0:T(8,128)(2,1)}), bf16[8,2,8,128]{3,2,1,0:T(8,128)(2,1)S(1)}, u32[]{:S(2)}, u32[]{:S(2)}) async-start(bf16[8,2,8,128]{3,2,1,0:T(8,128)(2,1)} %bitcast.12), calls=%async_computation | async-start | bytes 65536 | tf_op jit(solution)/shard_map/all_to_all | solution.py:134
  56.3 0.6 copy-done.24
  57.2 0.5 copy-done.12
  57.7 16.1 %all_gather.14 = bf16[64,128]{1,0:T(8,128)(2,1)S(1)} all-gather(bf16[8,128]{1,0:T(8,128)(2,1)S(1)} %slice.58), channel_id=1, replica_groups=mesh['seq'=4,'row'=4,'col'=2] {'seq','col'}, dimensions={0}, use_global_device_ids=true | all-gather | bytes 18432 | tf_op jit(solution)/shard_map/all_gather | solution.py:153
  73.9 1.3 %gather_fusion = bf16[512,128]{1,0:T(8,128)(2,1)S(1)} fusion(bf16[64,128]{1,0:T(8,128)(2,1)S(1)} %all_gather.14, s32[1024]{0:T(1024)S(1)} %pad_clamp_fusion), kind=kCustom, calls=%fused_computation | custom fusion | bytes 264192 | tf_op jit(solution)/shard_map/gather | solution.py:157
  75.5 0.5 slice-done
  76.1 0.6 copy-done.11
  76.8 15.5 %all-gather.2 = f32[8,8,3]{1,2,0:T(4,128)S(1)} all-gather(f32[1,8,3]{1,2,0:T(4,128)S(1)} %bitcast.152), channel_id=1, replica_groups=mesh['seq'=4,'row'=4,'col'=2] {'seq','col'}, dimensions={0}, use_global_device_ids=true | all-gather | bytes 864 | tf_op jit(solution)/shard_map/all_gather | solution.py:154
  92.4 1.0 gather_fusion.1
  96.0 0.7 fusion.39
  96.7 0.6 copy-done.10
  97.5 3.6 %while.10 = (s32[]{:T(128)}, bf16[2,64,128]{2,1,0:T(8,128)(2,1)S(1)}, bf16[2,64,128]{2,1,0:T(8,128)(2,1)S(1)}, f32[128]{0:T(128)S(1)}, bf16[128,512]{1,0:T(8,128...) while((s32[]{:T(128)}, bf16[2,64,128]{2,1,0:T(8,128)(2,1)S(1)}, bf16[2,64,128]{2,1,0:T(8,128)(2,1)S(1)}, ...), condition=%wide.region_8.9_spmd, body=%wide.region_3.8_spmd.sunk | while | flops 13935040 | bytes 1021277 | solution.py:132
  101.1 0.6 copy.98
  101.7 3.3 %all-to-all-start.1 = ((bf16[1,2,64,128]{3,1,0,2:T(2,128)(2,1)}), bf16[1,2,64,128]{3,1,0,2:T(2,128)(2,1)S(1)}, u32[]{:S(2)}, u32[]{:S(2)}) async-start(bf16[1,2,64,128]{3,1,0,2:T(2,128)(2,1)} %bitcast.104), calls=%async_computation.1 | async-start | bytes 65536 | tf_op jit(solution)/shard_map/all_to_all | solution.py:137
  105.3 0.7 copy.80
  105.9 3.8 %all-to-all-done.1 = bf16[1,2,64,128]{3,1,0,2:T(2,128)(2,1)S(1)} async-done(((bf16[1,2,64,128]{3,1,0,2:T(2,128)(2,1)}), bf16[1,2,64,128]{3,1,0,2:T(2,128)(2,1)S(1)}, u32[]{:S(2)}, u32[]{:S(2)}) %all-to-all-start.1) | async-done | bytes 32800 | tf_op jit(solution)/shard_map/all_to_all | solution.py:137
  109.7 0.6 copy.74
  (120 shorter events, 9.7 us)
Async XLA Ops:
  0.6 50.5 %copy-start = (bf16[1024,128]{1,0:T(8,128)(2,1)S(1)}, bf16[1024,128]{1,0:T(8,128)(2,1)}, u32[]{:S(2)}) copy-start(bf16[1024,128]{1,0:T(8,128)(2,1)} %param.34) | copy-start | bytes 786436
  0.7 0.7 copy-start.14
  0.7 0.8 copy-start.7
  0.7 0.8 copy-start.8
  1.7 0.7 copy-start.21
  17.3 19.0 %copy-start.22 = (bf16[64,32]{0,1:T(8,128)(2,1)S(1)}, bf16[64,32]{0,1:T(8,128)(2,1)}, u32[]{:S(2)}) copy-start(bf16[64,32]{0,1:T(8,128)(2,1)} %param.32) | copy-start | bytes 12292
  50.0 1.1 %copy-start.5 = (bf16[16,8,128]{2,1,0:T(8,128)(2,1)S(1)}, bf16[16,8,128]{2,1,0:T(8,128)(2,1)}, u32[]{:S(2)}) copy-start(bf16[16,8,128]{2,1,0:T(8,128)(2,1)} %param.36) | copy-start | bytes 98308
  50.1 1.1 %copy-start.16 = (f32[128]{0:T(128)S(1)}, f32[128]{0:T(128)}, u32[]{:S(2)}) copy-start(f32[128]{0:T(128)} %param.35) | copy-start | bytes 1540
  52.0 3.9 %copy-start.6 = (bf16[8,64]{1,0:T(8,128)(2,1)S(1)}, bf16[8,64]{1,0:T(8,128)(2,1)}, u32[]{:S(2)}) copy-start(bf16[8,64]{1,0:T(8,128)(2,1)} %param.43) | copy-start | bytes 3076
  52.0 4.2 %copy-start.18 = (bf16[64,64]{1,0:T(8,128)(2,1)S(1)}, bf16[64,64]{1,0:T(8,128)(2,1)}, u32[]{:S(2)}) copy-start(bf16[64,64]{1,0:T(8,128)(2,1)} %param.50) | copy-start | bytes 24580
  52.0 4.2 %copy-start.19 = (bf16[64,64]{1,0:T(8,128)(2,1)S(1)}, bf16[64,64]{1,0:T(8,128)(2,1)}, u32[]{:S(2)}) copy-start(bf16[64,64]{1,0:T(8,128)(2,1)} %param.49) | copy-start | bytes 24580
  52.0 4.2 %copy-start.20 = (bf16[64,64]{1,0:T(8,128)(2,1)S(1)}, bf16[64,64]{1,0:T(8,128)(2,1)}, u32[]{:S(2)}) copy-start(bf16[64,64]{1,0:T(8,128)(2,1)} %param.48) | copy-start | bytes 24580
  52.1 44.7 %all-to-all-start = ((bf16[8,2,8,128]{3,2,1,0:T(8,128)(2,1)}), bf16[8,2,8,128]{3,2,1,0:T(8,128)(2,1)S(1)}, u32[]{:S(2)}, u32[]{:S(2)}) async-start(bf16[8,2,8,128]{3,2,1,0:T(8,128)(2,1)} %bitcast.12), calls=%async_computation | async-start | bytes 65536 | tf_op jit(solution)/shard_map/all_to_all | solution.py:134
  57.7 16.1 %copy-start.13 = (s32[8,64]{1,0:T(8,128)S(1)}, s32[8,64]{1,0:T(8,128)}, u32[]{:S(2)}) copy-start(s32[8,64]{1,0:T(8,128)} %param.45) | copy-start | bytes 6148
  75.4 0.7 slice-start
  76.0 0.7 copy-start.11
  92.4 1.0 copy-start.25
  95.2 0.7 copy-start.9
  95.2 1.4 %copy-start.2 = (bf16[128,128]{1,0:T(8,128)(2,1)S(1)}, bf16[128,128]{1,0:T(8,128)(2,1)}, u32[]{:S(2)}) copy-start(bf16[128,128]{1,0:T(8,128)(2,1)} %param.40) | copy-start | bytes 98308
  95.2 1.4 %copy-start.3 = (bf16[128,128]{1,0:T(8,128)(2,1)S(1)}, bf16[128,128]{1,0:T(8,128)(2,1)}, u32[]{:S(2)}) copy-start(bf16[128,128]{1,0:T(8,128)(2,1)} %param.39) | copy-start | bytes 98308
  95.2 1.4 %copy-start.4 = (bf16[128,128]{1,0:T(8,128)(2,1)S(1)}, bf16[128,128]{1,0:T(8,128)(2,1)}, u32[]{:S(2)}) copy-start(bf16[128,128]{1,0:T(8,128)(2,1)} %param.38) | copy-start | bytes 98308
  95.4 1.2 %copy-start.1 = (bf16[128,128]{1,0:T(8,128)(2,1)S(1)}, bf16[128,128]{1,0:T(8,128)(2,1)}, u32[]{:S(2)}) copy-start(bf16[128,128]{1,0:T(8,128)(2,1)} %param.41) | copy-start | bytes 98308
  96.7 0.8 copy-start.17
  101.7 8.0 %all-to-all-start.1 = ((bf16[1,2,64,128]{3,1,0,2:T(2,128)(2,1)}), bf16[1,2,64,128]{3,1,0,2:T(2,128)(2,1)S(1)}, u32[]{:S(2)}, u32[]{:S(2)}) async-start(bf16[1,2,64,128]{3,1,0,2:T(2,128)(2,1)} %bitcast.104), calls=%async_computation.1 | async-start | bytes 65536 | tf_op jit(solution)/shard_map/all_to_all | solution.py:137
  (6 other events, 3.9 us)
where the time goes:
time: 111 us; the launch traced here: 110 us
  blocking collectives  77.5 us (70%)
  local copies, waits for them, and re-layouts  13.8 us (12%)
  starting transfers between devices  7.22 us (7%)
  matrix products  5.05 us (5%)
  waiting for transfers between devices  3.82 us (3%)
  other arithmetic  1.8 us (2%)
    psum x1, blocking collectives, spread(): return lax.psum(kept, axis)  19 us
    all_gather x1, blocking collectives, on_device(): lax.all_gather(key_value.astype(jnp.float32), ('seq', 'col'), axis=0, til...  16.1 us
    all_gather x1, blocking collectives, on_device(): lax.all_gather(coords, ('seq', 'col'), axis=1, tiled=True)  15.5 us
    all_gather x1, blocking collectives, on_device(): lax.all_gather(right_factor, ('seq', 'col'), axis=0, tiled=True)  14.4 us
    all_gather x1, blocking collectives, on_device(): lax.all_gather(left_factor, ('seq', 'col'), axis=0, tiled=True)  12.5 us
    unnamed x62, local copies, waits for them, and re-layouts  6.48 us
    all_to_all x1, starting transfers between devices, on_device(): lax.all_to_all(sectioned, ('seq', 'col'), split_axis=0, concat_axis=2, ti...  3.88 us
    all_to_all x1, waiting for transfers between devices, on_device(): lax.all_to_all(row_major, ('seq', 'col'), split_axis=2, concat_axis=0, ti...  3.82 us
  transfers between devices with their start and end apart: 2, of which 1 were waited for; matrix products, arithmetic and copies ran while one was open for 6% of the time, Pallas kernels for 0%

commit v1 on v0

v1 whole, which is shorter than its diff:
```python
import functools

import jax
import jax.numpy as jnp
from jax import lax
from jax.experimental import pallas as pl
from jax.experimental.pallas import tpu as pltpu
from jax.sharding import PartitionSpec as P

PAIR_HEADS = 4
NODE_HEADS = 4
F32 = jnp.float32
BF16 = jnp.bfloat16
MESH = pl.DeviceIdType.MESH


def dot(a, b, ca=1, cb=0):
    return lax.dot_general(a, b, (((ca,), (cb,)), ((), ())), preferred_element_type=F32)


def normalize(x, gain):
    centred = x - jnp.mean(x, -1, keepdims=True)
    variance = jnp.mean(centred * centred, -1, keepdims=True)
    return centred * lax.rsqrt(variance + 1e-05) * gain


def row_to_column(row, size):
    across = lax.broadcasted_iota(jnp.int32, (size, size), 1)
    down = lax.broadcasted_iota(jnp.int32, (size, size), 0)
    return jnp.sum(jnp.where(across == down, row, 0.0), 1, keepdims=True)


def head_of_lane(shape, heads):
    return lax.broadcasted_iota(jnp.int32, shape, 1) // (shape[1] // heads)


def kernel(
    axes,
    msa_hbm, ids_hbm, lookup_hbm, msa_gain_hbm, w_left_hbm, w_right_hbm, w_outer_hbm, bias_hbm,
    pair_hbm, pair_gain_hbm, wq_hbm, wk_hbm, wv_hbm, wg_hbm, wo_hbm,
    nodes_hbm, coords_hbm, index_hbm, count_hbm, node_gain_hbm, nq_hbm, nk_hbm, nv_hbm, no_hbm,
    penalty_hbm, step_hbm,
    pair_out, nodes_out, coords_out,
    msa, ids, lookup, msa_gain, w_left, w_right, w_outer, bias, pair_gain, w_proj, wo,
    nodes, coords, index, count, node_gain, nw, no, penalty, step,
    pair_all, left_send, left_all, right_all, node_all, w_wide, w_flat, t_all, out_send,
    load_sem, send_sem, recv_sem, own_sem,
):
    n_seq, n_row, n_col = axes
    groups = n_seq * n_col
    seq, row, col = lax.axis_index("seq"), lax.axis_index("row"), lax.axis_index("col")
    g = seq * n_col + col
    seqs, rows_i, width_in = msa.shape
    product = w_left.shape[0]
    block = pair_all.shape[1]
    channels = wo.shape[0]
    rows_own = rows_i // groups
    cols = block // rows_own
    length = cols * groups
    total = seqs * groups

    def device(r, q):
        return (q // n_col, r, q % n_col)

    def others(position, size, body):
        def one(k, carry):
            body(lax.rem(position + k, size))
            return carry
        lax.fori_loop(1, size, one, 0, unroll=size <= 8)

    def group(body):
        others(g, groups, body)

    def rows_of_mesh(body):
        others(row, n_row, body)

    barrier = pltpu.get_barrier_semaphore()

    def greet(r, q):
        pl.semaphore_signal(barrier, inc=1, device_id=device(r, q), device_id_type=MESH)

    rows_of_mesh(lambda r: greet(r, g))
    group(lambda q: greet(row, q))

    def load(slot, source, target):
        copy = pltpu.make_async_copy(source, target, load_sem.at[slot])
        copy.start()
        return copy

    msa_loads = [
        load(0, ids_hbm, ids), load(1, msa_hbm, msa), load(2, lookup_hbm, lookup),
        load(3, msa_gain_hbm, msa_gain), load(4, w_left_hbm, w_left), load(5, w_right_hbm, w_right),
    ]
    node_loads = [load(6, nodes_hbm, nodes), load(7, coords_hbm, coords)]
    outer_loads = [load(8, w_outer_hbm, w_outer)]
    node_width = node_gain.shape[1]
    later_loads = [
        load(9, index_hbm, index), load(10, count_hbm, count), load(11, node_gain_hbm, node_gain),
        load(12, nq_hbm, nw.at[0]), load(13, nk_hbm, nw.at[1]), load(14, nv_hbm, nw.at[2]),
        load(15, no_hbm, no), load(16, penalty_hbm, penalty), load(17, step_hbm, step),
    ]
    pair_loads = [
        load(18, bias_hbm, bias), load(19, pair_gain_hbm, pair_gain),
        load(20, wq_hbm, w_proj.at[0]), load(21, wk_hbm, w_proj.at[1]),
        load(22, wv_hbm, w_proj.at[2]), load(23, wg_hbm, w_proj.at[3]), load(24, wo_hbm, wo),
    ]
    own_pair = pltpu.make_async_copy(pair_hbm.at[g], pair_all.at[g], own_sem.at[0])
    own_pair.start()

    for copy in msa_loads:
        copy.wait()
    kinds = lookup.shape[1]
    hot = []
    for s in range(seqs):
        column = row_to_column(ids[s : s + 1, :].astype(F32), rows_i).astype(jnp.int32)
        hot.append(column == lax.broadcasted_iota(jnp.int32, (rows_i, kinds), 1))
    hot = jnp.concatenate([h.astype(F32) for h in hot], 0).astype(BF16)
    embedded = dot(hot, lookup[...], 1, 1)
    msa_in = msa[...].astype(F32).reshape(seqs * rows_i, width_in) + embedded
    msa_norm = normalize(msa_in, msa_gain[...]).astype(BF16)
    left = dot(msa_norm, w_left[...], 1, 1).astype(BF16).astype(F32)
    right = dot(msa_norm, w_right[...], 1, 1)
    right_all[g * n_row + row] = jnp.concatenate(
        [right[s * rows_i : (s + 1) * rows_i] for s in range(seqs)], 1
    ).astype(BF16)
    for s in range(seqs):
        left_send[pl.ds(s, rows_i, stride=seqs), :] = left[s * rows_i : (s + 1) * rows_i]
    slab = rows_own * seqs
    left_all[g] = left_send[pl.ds(pl.multiple_of(g * slab, slab), slab), :]

    for copy in node_loads:
        copy.wait()
    local = nodes.shape[0]
    node_all[g] = jnp.concatenate(
        [nodes[...].astype(F32)]
        + [row_to_column(coords[x : x + 1, :], local) for x in range(3)]
        + [jnp.zeros((local, node_all.shape[2] - node_width - 3), F32)],
        1,
    )

    pl.semaphore_wait(barrier, n_row - 1 + groups - 1)

    def send(source, target, kind, r, q):
        pltpu.make_async_remote_copy(
            src_ref=source, dst_ref=target, send_sem=send_sem.at[kind], recv_sem=recv_sem.at[kind],
            device_id=device(r, q), device_id_type=MESH,
        ).start()

    mine = right_all.at[g * n_row + row]
    rows_of_mesh(lambda r: send(mine, mine, 5, r, g))
    group(lambda q: send(
        left_send.at[pl.ds(pl.multiple_of(q * slab, slab), slab)], left_all.at[g], 1, row, q
    ))
    group(lambda q: send(node_all.at[g], node_all.at[g], 3, row, q))
    group(lambda q: send(pair_hbm.at[q], pair_all.at[g], 2, row, q))

    def wait_bytes(ref, sem):
        pltpu.make_async_copy(ref, ref, sem).wait()

    for copy in outer_loads:
        copy.wait()
    w_flat[...] = w_outer[...].astype(F32)
    for d in range(product):
        w_wide[:, d * channels : (d + 1) * channels] = w_flat[
            pl.ds(d, product, stride=product), :
        ].astype(BF16)

    wait_bytes(right_all.at[pl.ds(0, n_row - 1)], recv_sem.at[5])
    gathered = right_all.at[pl.ds(g * n_row, n_row)]
    group(lambda q: send(gathered, gathered, 0, row, q))

    for copy in later_loads:
        copy.wait()
    slots = index.shape[1]
    counted = row_to_column(count[...].astype(F32), local)
    lane = lax.broadcasted_iota(jnp.int32, (local, slots), 1)
    live_index = jnp.where(lane.astype(F32) < counted, index[...], -1)
    everyone_n = lax.broadcasted_iota(jnp.int32, (local, length), 1)
    times = jnp.zeros((local, length), F32)
    for t in range(slots):
        times = times + jnp.where(live_index[:, t : t + 1] == everyone_n, 1.0, 0.0)
    wait_bytes(node_all.at[pl.ds(0, groups - 1)], recv_sem.at[3])
    table = node_all[...].reshape(length, node_all.shape[2])
    own = node_all[g]
    node_x = normalize(table[:, :node_width], node_gain[...]).astype(BF16)
    own_x = normalize(own[:, :node_width], node_gain[...]).astype(BF16)
    node_query = dot(own_x, nw[0])
    node_key = dot(node_x, nw[1]).astype(BF16)
    node_value = dot(node_x, nw[2]).astype(BF16)
    turned = table.T
    offsets = [
        turned[node_width + x : node_width + x + 1, :] - own[:, node_width + x : node_width + x + 1]
        for x in range(3)
    ]
    dist2 = offsets[0] * offsets[0] + offsets[1] * offsets[1] + offsets[2] * offsets[2]
    node_head = head_of_lane((local, node_width), NODE_HEADS)
    query_rows = jnp.concatenate(
        [jnp.where(node_head == h, node_query, 0.0) for h in range(NODE_HEADS)], 0
    ).astype(BF16)
    logits = dot(query_rows, node_key, 1, 1) * (node_width // NODE_HEADS) ** (-0.5)
    weighted = []
    pull = jnp.zeros((local, length), F32)
    for h in range(NODE_HEADS):
        rows = logits[h * local : (h + 1) * local] - penalty[:, h : h + 1] * dist2
        rows = jnp.where(times > 0.0, rows, -1e30)
        raised = times * jnp.exp(rows - jnp.max(rows, 1, keepdims=True))
        part = raised / jnp.sum(raised, 1, keepdims=True)
        weighted.append(part)
        pull = pull + step[:, h : h + 1] * part
    mixed = dot(jnp.concatenate(weighted, 0).astype(BF16), node_value)
    node_mix = jnp.zeros((local, node_width), F32)
    for h in range(NODE_HEADS):
        node_mix = jnp.where(node_head == h, mixed[h * local : (h + 1) * local], node_mix)
    nodes_out[...] = (nodes[...].astype(F32) + dot(node_mix.astype(BF16), no[...])).astype(BF16)
    down = lax.broadcasted_iota(jnp.int32, (local, local), 0)
    across = lax.broadcasted_iota(jnp.int32, (local, local), 1)
    moved = [
        jnp.sum(jnp.where(down == across, jnp.sum(offsets[x] * pull, 1, keepdims=True), 0.0), 0, keepdims=True)
        for x in range(3)
    ]
    coords_out[...] = coords[...] + jnp.concatenate(moved, 0)

    wait_bytes(left_all.at[pl.ds(0, groups - 1)], recv_sem.at[1])
    left_rows = left_all[...].reshape(groups * slab, product).astype(BF16)
    t_rows = dot(left_rows, w_wide[...]) * (1.0 / total)
    for d in range(product):
        t_all[pl.ds(d, groups * slab, stride=product), :] = t_rows[:, d * channels : (d + 1) * channels]
    deep = seqs * product
    t_pieces = [
        jnp.concatenate(
            [t_all[(q * rows_own + i) * deep : (q * rows_own + i + 1) * deep, :] for q in range(groups)], 0
        )
        for i in range(rows_own)
    ]
    t_joined = jnp.concatenate(t_pieces, 1).astype(BF16)
    own_pair.wait()
    wait_bytes(pair_all.at[pl.ds(0, groups - 1)], recv_sem.at[2])
    for copy in pair_loads:
        copy.wait()
    old = pair_all[...].astype(F32)
    wait_bytes(right_all.at[pl.ds(0, n_row * (groups - 1))], recv_sem.at[0])
    right_rows = jnp.concatenate(
        [right_all[q * n_row : (q + 1) * n_row].reshape(length, deep) for q in range(groups)], 1
    )
    update = dot(right_rows, t_joined)
    mid = jnp.concatenate(
        [
            jnp.concatenate([old[q, i * cols : (i + 1) * cols] for q in range(groups)], 0)
            + update[:, i * channels : (i + 1) * channels]
            for i in range(rows_own)
        ],
        0,
    )
    mid = (mid + bias[...]).astype(BF16).astype(F32)

    normed = normalize(mid, pair_gain[...]).astype(BF16)
    queries = dot(normed, w_proj[0])
    keys = dot(normed, w_proj[1]).astype(BF16)
    values = dot(normed, w_proj[2]).astype(BF16)
    gates = dot(normed, w_proj[3])
    head = head_of_lane((length, channels), PAIR_HEADS)
    scale = (channels // PAIR_HEADS) ** (-0.5)
    joined = []
    for i in range(rows_own):
        at = slice(i * length, (i + 1) * length)
        spread = jnp.concatenate(
            [jnp.where(head == h, queries[at], 0.0) for h in range(PAIR_HEADS)], 0
        ).astype(BF16)
        scores = dot(keys[at], spread, 1, 1) * scale
        raised = jnp.exp(scores - jnp.max(scores, 0, keepdims=True))
        weights = (raised * (1.0 / jnp.sum(raised, 0, keepdims=True))).astype(BF16)
        heads = dot(weights, values[at], 0, 0)
        taken = heads[:length]
        for h in range(1, PAIR_HEADS):
            taken = jnp.where(head == h, heads[h * length : (h + 1) * length], taken)
        joined.append(taken)
    attended = jnp.concatenate(joined, 0) * (1.0 / (1.0 + jnp.exp(-gates)))
    result = mid + dot(attended.astype(BF16), wo[...])
    for q in range(groups):
        out_send[q] = jnp.concatenate(
            [result[i * length + q * cols : i * length + (q + 1) * cols] for i in range(rows_own)], 0
        ).astype(BF16)

    group(lambda q: send(out_send.at[q], pair_out.at[g], 4, row, q))
    pair_out[g] = out_send[g]
    wait_bytes(right_all.at[pl.ds(0, n_row - 1)], send_sem.at[5])
    wait_bytes(right_all.at[pl.ds(0, n_row * (groups - 1))], send_sem.at[0])
    wait_bytes(left_all.at[pl.ds(0, groups - 1)], send_sem.at[1])
    wait_bytes(pair_all.at[pl.ds(0, groups - 1)], send_sem.at[2])
    wait_bytes(node_all.at[pl.ds(0, groups - 1)], send_sem.at[3])
    wait_bytes(out_send.at[pl.ds(0, groups - 1)], send_sem.at[4])
    wait_bytes(out_send.at[pl.ds(0, groups - 1)], recv_sem.at[4])


def hand_over(*refs):
    sources, targets, sem = refs[:3], refs[3:6], refs[6]
    copies = [pltpu.make_async_copy(a, b, sem.at[k]) for k, (a, b) in enumerate(zip(sources, targets))]
    for copy in copies:
        copy.start()
    for copy in copies:
        copy.wait()


def on_device(axes, *args):
    (msa, ids, lookup, msa_gain, w_left, w_right, w_outer, bias, pair, pair_gain, wq, wk, wv, wg, wo,
     nodes, coords, index, count, node_gain, nq, nk, nv, no, penalty, step) = args
    groups = axes[0] * axes[2]
    n = groups * axes[1]
    seqs, rows_i, width_in = msa.shape
    _, cols, channels = pair.shape
    rows_own = rows_i // groups
    block = rows_own * cols
    product = w_left.shape[1]
    lookup, w_left, w_right = lookup.T, w_left.T, w_right.T
    local, node_width = nodes.shape
    slab = rows_own * seqs
    as_row = lambda x: x.reshape(1, -1)
    vmem = lambda x: pltpu.VMEM(x.shape, x.dtype)
    msa_gain, bias, pair_gain, count, node_gain, penalty, step = map(
        as_row, (msa_gain, bias, pair_gain, count, node_gain, penalty, step)
    )
    pair = pair.reshape(groups, block, channels)
    operands = (msa, ids, lookup, msa_gain, w_left, w_right, w_outer, bias, pair, pair_gain, wq, wk, wv,
                wg, wo, nodes, coords, index, count, node_gain, nq, nk, nv, no, penalty, step)
    scratch = [vmem(x) for x in (msa, ids, lookup, msa_gain, w_left, w_right, w_outer, bias, pair_gain)]
    scratch += [pltpu.VMEM((4, channels, channels), BF16), vmem(wo)]
    scratch += [vmem(x) for x in (nodes, coords, index, count, node_gain)]
    scratch += [pltpu.VMEM((3, node_width, node_width), BF16), vmem(no), vmem(penalty), vmem(step)]
    scratch += [
        pltpu.VMEM((groups, block, channels), BF16),
        pltpu.VMEM((groups * slab, product), F32),
        pltpu.VMEM((groups, slab, product), F32),
        pltpu.VMEM((n, rows_i, seqs * product), BF16),
        pltpu.VMEM((groups, local, 128), F32),
        pltpu.VMEM((product, product * channels), BF16),
        pltpu.VMEM((product * product, channels), F32),
        pltpu.VMEM((groups * slab * product, channels), F32),
        pltpu.VMEM((groups, block, channels), BF16),
        pltpu.SemaphoreType.DMA((25,)),
        pltpu.SemaphoreType.DMA((6,)),
        pltpu.SemaphoreType.DMA((6,)),
        pltpu.SemaphoreType.DMA((1,)),
    ]
    hbm = pl.BlockSpec(memory_space=pl.ANY)
    results = pl.pallas_call(
        functools.partial(kernel, axes),
        out_shape=[
            pltpu.VMEM(pair.shape, BF16),
            pltpu.VMEM(nodes.shape, BF16),
            pltpu.VMEM(coords.shape, F32),
        ],
        in_specs=[hbm] * len(operands),
        out_specs=[pl.BlockSpec(memory_space=pltpu.VMEM)] * 3,
        scratch_shapes=scratch,
        compiler_params=pltpu.CompilerParams(
            collective_id=0, has_side_effects=True, vmem_limit_bytes=56 * 1024 * 1024
        ),
    )(*operands)
    pair_out, nodes_out, coords_out = pl.pallas_call(
        hand_over,
        out_shape=[jax.ShapeDtypeStruct(x.shape, x.dtype) for x in results],
        in_specs=[pl.BlockSpec(memory_space=pltpu.VMEM)] * 3,
        out_specs=[hbm] * 3,
        scratch_shapes=[pltpu.SemaphoreType.DMA((3,))],
    )(*results)
    return pair_out.reshape(rows_i, cols, channels), nodes_out, coords_out


def solution(mesh):
    axes = (mesh.shape["seq"], mesh.shape["row"], mesh.shape["col"])
    both = ("seq", "col")
    placed = (
        (P(both, "row", None), P(both, "row"))
        + (P(),) * 6
        + (P("row", both, None),)
        + (P(),) * 6
        + (P(both, None), P(None, both), P(both, None), P(both))
        + (P(),) * 7
    )
    return jax.shard_map(
        functools.partial(on_device, axes),
        mesh=mesh,
        in_specs=placed,
        out_specs=(P("row", both, None), P(both, None), P(None, both)),
        check_vma=False,
    )
```

time: 111 us -> 21.3 us (0.19)
  blocking collectives: 77.5 us -> 0 us
  Pallas kernels: 0 us -> 18.7 us
  local copies, waits for them, and re-layouts: 13.8 us -> 1.78 us
  starting transfers between devices: 7.22 us -> 0 us
  matrix products: 5.05 us -> 0 us
  waiting for transfers between devices: 3.82 us -> 0 us
  other arithmetic: 1.8 us -> 0 us
    all_gather x4 -> x0, blocking collectives: 58.5 us -> none  [the longest x1 16.1 us: on_device(): lax.all_gather(key_value.astype(jnp.float32), ('seq', 'col'), axis=0, til...]
    psum x1 -> x0, blocking collectives: 19 us -> none  [spread(): return lax.psum(kept, axis)]
    pallas_call x0 -> x2, Pallas kernels: none -> 18.7 us  [the longest x1 17.3 us: on_device(): pl.pallas_call(functools.partial(kernel, axes), out_shape=[pltpu.VMEM(pai...]
    all_to_all x2 -> x0, starting transfers between devices: 7.22 us -> none  [the longest x1 3.88 us: on_device(): lax.all_to_all(sectioned, ('seq', 'col'), split_axis=0, concat_axis=2, ti...]
    unnamed x62 -> x6, local copies, waits for them, and re-layouts: 6.48 us -> 1.78 us
    dot_general x17 -> x0, matrix products: 4.53 us -> none  [the longest x1 0.84 us: on_device(): jnp.dot(outer, outer_output_weight, preferred_element_type=jnp.float32)]
    all_to_all x2 -> x0, waiting for transfers between devices: 3.82 us -> none  [the longest x1 3.82 us: on_device(): lax.all_to_all(row_major, ('seq', 'col'), split_axis=2, concat_axis=0, ti...]
    gather x2 -> x0, local copies, waits for them, and re-layouts: 2.37 us -> none  [the longest x1 1.33 us: on_device(): neighbour_rows = node_table[neighbour_index]]
  transfers between devices with their start and end apart: 2 -> 0, of which waited for: 1 -> 0; matrix products, arithmetic and copies ran while one was open for 6% -> 0% of each run, Pallas kernels for 0% -> 0%
where the time goes in v1:
time: 21.3 us; the launch traced here: 21.1 us
  Pallas kernels  18.7 us (88%)
  local copies, waits for them, and re-layouts  1.78 us (8%)
  between operations  0.66 us (3%)
    pallas_call x1, Pallas kernels, on_device(): pl.pallas_call(functools.partial(kernel, axes), out_shape=[pltpu.VMEM(pai...  17.3 us
    unnamed x6, local copies, waits for them, and re-layouts  1.78 us
    pallas_call x1, Pallas kernels, on_device(): pl.pallas_call(hand_over, out_shape=[jax.ShapeDtypeStruct(x.shape, x.dtyp...  1.41 us

profile of v1, /device:TPU:0, one launch (start us, length us, event | category | flops | bytes accessed | tf_op | source)
XLA Modules:
  0.0 21.1 jit_solution(16461108187484919476)
XLA Ops:
  0.6 17.3 %shard_map.265 = (bf16[8,16,128]{2,1,0:T(8,128)(2,1)S(1)}, bf16[8,64]{1,0:T(8,128)(2,1)S(1)}, f32[3,8]{1,0:T(4,128)S(1)}) custom-call(bf16[4,16,64]{2,1,0:T(8,128)(2,1)} %msa_hbm.1, s32[4,16]{1,0:T(4,128)} %ids_hbm.1, bf16[64,80]{1,0:T(8,128)(2,1)} %bitcast.13, f32[1,64]{1,0:T(1,128)} %bitcast.16, bf16[32,64]{1,0:T(8,128)(2,1)} %bitcast.14, ...), custom_call_target="tpu_custom_call" | custom-call | tf_op jit(solution)/shard_map/pallas_call | solution.py:345
  17.9 0.0 copy-start
  17.9 0.6 %copy-done = bf16[8,16,128]{2,1,0:T(8,128)(2,1)} copy-done((bf16[8,16,128]{2,1,0:T(8,128)(2,1)}, bf16[8,16,128]{2,1,0:T(8,128)(2,1)S(1)}, u32[]{:S(2)}) %copy-start) | copy-done | bytes 32792
  18.5 0.0 copy-start.1
  18.5 0.6 %copy-done.1 = bf16[8,64]{1,0:T(8,128)(2,1)} copy-done((bf16[8,64]{1,0:T(8,128)(2,1)}, bf16[8,64]{1,0:T(8,128)(2,1)S(1)}, u32[]{:S(2)}) %copy-start.1) | copy-done | bytes 1048
  19.1 0.0 copy-start.2
  19.1 0.6 %copy-done.2 = f32[3,8]{1,0:T(4,128)} copy-done((f32[3,8]{1,0:T(4,128)}, f32[3,8]{1,0:T(4,128)S(1)}, u32[]{:S(2)}) %copy-start.2) | copy-done | bytes 120
  19.7 1.4 %shard_map.266 = (bf16[8,16,128]{2,1,0:T(8,128)(2,1)}, bf16[8,64]{1,0:T(8,128)(2,1)}, f32[3,8]{1,0:T(4,128)}) custom-call(bf16[8,16,128]{2,1,0:T(8,128)(2,1)} %copy-done, bf16[8,64]{1,0:T(8,128)(2,1)} %copy-done.1, f32[3,8]{1,0:T(4,128)} %copy-done.2), custom_call_target="tpu_custom_call" | custom-call | tf_op jit(solution)/shard_map/pallas_call | solution.py:359
Async XLA Ops:
  17.9 0.6 %copy-start = (bf16[8,16,128]{2,1,0:T(8,128)(2,1)}, bf16[8,16,128]{2,1,0:T(8,128)(2,1)S(1)}, u32[]{:S(2)}) copy-start(bf16[8,16,128]{2,1,0:T(8,128)(2,1)S(1)} %get-tuple-element.9.refs_0_) | copy-start | bytes 98308
  18.5 0.6 %copy-start.1 = (bf16[8,64]{1,0:T(8,128)(2,1)}, bf16[8,64]{1,0:T(8,128)(2,1)S(1)}, u32[]{:S(2)}) copy-start(bf16[8,64]{1,0:T(8,128)(2,1)S(1)} %get-tuple-element.10.refs_1_) | copy-start | bytes 3076
  19.1 0.6 %copy-start.2 = (f32[3,8]{1,0:T(4,128)}, f32[3,8]{1,0:T(4,128)S(1)}, u32[]{:S(2)}) copy-start(f32[3,8]{1,0:T(4,128)S(1)} %get-tuple-element.11.refs_2_) | copy-start | bytes 292

commit v2 on v1

--- a/solution.py
+++ b/solution.py
@@ -165,10 +165,6 @@
             pl.ds(d, product, stride=product), :
         ].astype(BF16)
 
-    wait_bytes(right_all.at[pl.ds(0, n_row - 1)], recv_sem.at[5])
-    gathered = right_all.at[pl.ds(g * n_row, n_row)]
-    group(lambda q: send(gathered, gathered, 0, row, q))
-
     for copy in later_loads:
         copy.wait()
     slots = index.shape[1]
@@ -179,6 +175,25 @@
     times = jnp.zeros((local, length), F32)
     for t in range(slots):
         times = times + jnp.where(live_index[:, t : t + 1] == everyone_n, 1.0, 0.0)
+
+    wait_bytes(right_all.at[pl.ds(0, n_row - 1)], recv_sem.at[5])
+    gathered = right_all.at[pl.ds(g * n_row, n_row)]
+    group(lambda q: send(gathered, gathered, 0, row, q))
+
+    wait_bytes(left_all.at[pl.ds(0, groups - 1)], recv_sem.at[1])
+    left_rows = left_all[...].reshape(groups * slab, product).astype(BF16)
+    t_rows = dot(left_rows, w_wide[...]) * (1.0 / total)
+    for d in range(product):
+        t_all[pl.ds(d, groups * slab, stride=product), :] = t_rows[:, d * channels : (d + 1) * channels]
+    deep = seqs * product
+    t_pieces = [
+        jnp.concatenate(
+            [t_all[(q * rows_own + i) * deep : (q * rows_own + i + 1) * deep, :] for q in range(groups)], 0
+        )
+        for i in range(rows_own)
+    ]
+    t_joined = jnp.concatenate(t_pieces, 1).astype(BF16)
+
     wait_bytes(node_all.at[pl.ds(0, groups - 1)], recv_sem.at[3])
     table = node_all[...].reshape(length, node_all.shape[2])
     own = node_all[g]
@@ -193,46 +208,6 @@
         for x in range(3)
     ]
     dist2 = offsets[0] * offsets[0] + offsets[1] * offsets[1] + offsets[2] * offsets[2]
-    node_head = head_of_lane((local, node_width), NODE_HEADS)
-    query_rows = jnp.concatenate(
-        [jnp.where(node_head == h, node_query, 0.0) for h in range(NODE_HEADS)], 0
-    ).astype(BF16)
-    logits = dot(query_rows, node_key, 1, 1) * (node_width // NODE_HEADS) ** (-0.5)
-    weighted = []
-    pull = jnp.zeros((local, length), F32)
-    for h in range(NODE_HEADS):
-        rows = logits[h * local : (h + 1) * local] - penalty[:, h : h + 1] * dist2
-        rows = jnp.where(times > 0.0, rows, -1e30)
-        raised = times * jnp.exp(rows - jnp.max(rows, 1, keepdims=True))
-        part = raised / jnp.sum(raised, 1, keepdims=True)
-        weighted.append(part)
-        pull = pull + step[:, h : h + 1] * part
-    mixed = dot(jnp.concatenate(weighted, 0).astype(BF16), node_value)
-    node_mix = jnp.zeros((local, node_width), F32)
-    for h in range(NODE_HEADS):
-        node_mix = jnp.where(node_head == h, mixed[h * local : (h + 1) * local], node_mix)
-    nodes_out[...] = (nodes[...].astype(F32) + dot(node_mix.astype(BF16), no[...])).astype(BF16)
-    down = lax.broadcasted_iota(jnp.int32, (local, local), 0)
-    across = lax.broadcasted_iota(jnp.int32, (local, local), 1)
-    moved = [
-        jnp.sum(jnp.where(down == across, jnp.sum(offsets[x] * pull, 1, keepdims=True), 0.0), 0, keepdims=True)
-        for x in range(3)
-    ]
-    coords_out[...] = coords[...] + jnp.concatenate(moved, 0)
-
-    wait_bytes(left_all.at[pl.ds(0, groups - 1)], recv_sem.at[1])
-    left_rows = left_all[...].reshape(groups * slab, product).astype(BF16)
-    t_rows = dot(left_rows, w_wide[...]) * (1.0 / total)
-    for d in range(product):
-        t_all[pl.ds(d, groups * slab, stride=product), :] = t_rows[:, d * channels : (d + 1) * channels]
-    deep = seqs * product
-    t_pieces = [
-        jnp.concatenate(
-            [t_all[(q * rows_own + i) * deep : (q * rows_own + i + 1) * deep, :] for q in range(groups)], 0
-        )
-        for i in range(rows_own)
-    ]
-    t_joined = jnp.concatenate(t_pieces, 1).astype(BF16)
     own_pair.wait()
     wait_bytes(pair_all.at[pl.ds(0, groups - 1)], recv_sem.at[2])
     for copy in pair_loads:
@@ -283,6 +258,33 @@
 
     group(lambda q: send(out_send.at[q], pair_out.at[g], 4, row, q))
     pair_out[g] = out_send[g]
+    node_head = head_of_lane((local, node_width), NODE_HEADS)
+    query_rows = jnp.concatenate(
+        [jnp.where(node_head == h, node_query, 0.0) for h in range(NODE_HEADS)], 0
+    ).astype(BF16)
+    logits = dot(query_rows, node_key, 1, 1) * (node_width // NODE_HEADS) ** (-0.5)
+    weighted = []
+    pull = jnp.zeros((local, length), F32)
+    for h in range(NODE_HEADS):
+        rows = logits[h * local : (h + 1) * local] - penalty[:, h : h + 1] * dist2
+        rows = jnp.where(times > 0.0, rows, -1e30)
+        raised = times * jnp.exp(rows - jnp.max(rows, 1, keepdims=True))
+        part = raised / jnp.sum(raised, 1, keepdims=True)
+        weighted.append(part)
+        pull = pull + step[:, h : h + 1] * part
+    mixed = dot(jnp.concatenate(weighted, 0).astype(BF16), node_value)
+    node_mix = jnp.zeros((local, node_width), F32)
+    for h in range(NODE_HEADS):
+        node_mix = jnp.where(node_head == h, mixed[h * local : (h + 1) * local], node_mix)
+    nodes_out[...] = (nodes[...].astype(F32) + dot(node_mix.astype(BF16), no[...])).astype(BF16)
+    down = lax.broadcasted_iota(jnp.int32, (local, local), 0)
+    across = lax.broadcasted_iota(jnp.int32, (local, local), 1)
+    moved = [
+        jnp.sum(jnp.where(down == across, jnp.sum(offsets[x] * pull, 1, keepdims=True), 0.0), 0, keepdims=True)
+        for x in range(3)
+    ]
+    coords_out[...] = coords[...] + jnp.concatenate(moved, 0)
+
     wait_bytes(right_all.at[pl.ds(0, n_row - 1)], send_sem.at[5])
     wait_bytes(right_all.at[pl.ds(0, n_row * (groups - 1))], send_sem.at[0])
     wait_bytes(left_all.at[pl.ds(0, groups - 1)], send_sem.at[1])
@@ -362,6 +364,7 @@
         in_specs=[pl.BlockSpec(memory_space=pltpu.VMEM)] * 3,
         out_specs=[hbm] * 3,
         scratch_shapes=[pltpu.SemaphoreType.DMA((3,))],
+        compiler_params=pltpu.CompilerParams(vmem_limit_bytes=1024 * 1024),
     )(*results)
     return pair_out.reshape(rows_i, cols, channels), nodes_out, coords_out
 

time: 21.3 us -> 18.7 us (0.88)
  local copies, waits for them, and re-layouts: 1.78 us -> 0 us
  Pallas kernels: 18.7 us -> 17.9 us
    unnamed x6 -> x0, local copies, waits for them, and re-layouts: 1.78 us -> none
    pallas_call x1, Pallas kernels: 1.41 us -> 0.65 us  [on_device(): pl.pallas_call(hand_over, out_shape=[jax.ShapeDtypeStruct(x.shape, x.dtyp...]
where the time goes in v2:
time: 18.7 us; the launch traced here: 18.6 us
  Pallas kernels  17.9 us (96%)
  between operations  0.65 us (3%)
    pallas_call x1, Pallas kernels, on_device(): pl.pallas_call(functools.partial(kernel, axes), out_shape=[pltpu.VMEM(pai...  17.3 us
    pallas_call x1, Pallas kernels, on_device(): pl.pallas_call(hand_over, out_shape=[jax.ShapeDtypeStruct(x.shape, x.dtyp...  0.65 us

profile of v2, /device:TPU:0, one launch (start us, length us, event | category | flops | bytes accessed | tf_op | source)
XLA Modules:
  0.0 18.6 jit_solution(11989203258847228977)
XLA Ops:
  0.6 17.3 %shard_map.265 = (bf16[8,16,128]{2,1,0:T(8,128)(2,1)S(1)}, bf16[8,64]{1,0:T(8,128)(2,1)S(1)}, f32[3,8]{1,0:T(4,128)S(1)}) custom-call(bf16[4,16,64]{2,1,0:T(8,128)(2,1)} %msa_hbm.1, s32[4,16]{1,0:T(4,128)} %ids_hbm.1, bf16[64,80]{1,0:T(8,128)(2,1)} %bitcast.13, f32[1,64]{1,0:T(1,128)} %bitcast.16, bf16[32,64]{1,0:T(8,128)(2,1)} %bitcast.14, ...), custom_call_target="tpu_custom_call" | custom-call | tf_op jit(solution)/shard_map/pallas_call | solution.py:347
  17.9 0.6 %shard_map.266 = (bf16[8,16,128]{2,1,0:T(8,128)(2,1)}, bf16[8,64]{1,0:T(8,128)(2,1)}, f32[3,8]{1,0:T(4,128)}) custom-call(bf16[8,16,128]{2,1,0:T(8,128)(2,1)S(1)} %get-tuple-element.9.refs_0_, bf16[8,64]{1,0:T(8,128)(2,1)S(1)} %get-tuple-element.10.refs_1_, f32[3,8]{1,0:T(4,128)S(1)} %get-tuple-element.11.refs_2_), custom_call_target="tpu_custom_call" | custom-call | tf_op jit(solution)/shard_map/pallas_call | solution.py:361

commit v3 on v2

--- a/solution.py
+++ b/solution.py
@@ -71,16 +71,16 @@
     def group(body):
         others(g, groups, body)
 
-    def rows_of_mesh(body):
-        others(row, n_row, body)
+    toward = jnp.where(2 * row < n_row, 1, n_row - 1)
+
+    def rows_of_mesh(body, far_first=False):
+        for k in range(1, n_row):
+            body(lax.rem(row + (n_row - k if far_first else k) * toward, n_row))
 
     barrier = pltpu.get_barrier_semaphore()
 
     def greet(r, q):
         pl.semaphore_signal(barrier, inc=1, device_id=device(r, q), device_id_type=MESH)
-
-    rows_of_mesh(lambda r: greet(r, g))
-    group(lambda q: greet(row, q))
 
     def load(slot, source, target):
         copy = pltpu.make_async_copy(source, target, load_sem.at[slot])
@@ -91,6 +91,8 @@
         load(0, ids_hbm, ids), load(1, msa_hbm, msa), load(2, lookup_hbm, lookup),
         load(3, msa_gain_hbm, msa_gain), load(4, w_left_hbm, w_left), load(5, w_right_hbm, w_right),
     ]
+    rows_of_mesh(lambda r: greet(r, g))
+    group(lambda q: greet(row, q))
     node_loads = [load(6, nodes_hbm, nodes), load(7, coords_hbm, coords)]
     outer_loads = [load(8, w_outer_hbm, w_outer)]
     node_width = node_gain.shape[1]
@@ -140,14 +142,16 @@
 
     pl.semaphore_wait(barrier, n_row - 1 + groups - 1)
 
-    def send(source, target, kind, r, q):
+    def send(source, target, kind, r, q, arrival=None):
         pltpu.make_async_remote_copy(
-            src_ref=source, dst_ref=target, send_sem=send_sem.at[kind], recv_sem=recv_sem.at[kind],
+            src_ref=source, dst_ref=target, send_sem=send_sem.at[kind],
+            recv_sem=recv_sem.at[kind if arrival is None else arrival],
             device_id=device(r, q), device_id_type=MESH,
         ).start()
 
     mine = right_all.at[g * n_row + row]
-    rows_of_mesh(lambda r: send(mine, mine, 5, r, g))
+    rows_of_mesh(lambda r: send(mine, mine, 5, r, g, 5 + row), far_first=True)
+    group(lambda q: send(mine, mine, 0, row, q))
     group(lambda q: send(
         left_send.at[pl.ds(pl.multiple_of(q * slab, slab), slab)], left_all.at[g], 1, row, q
     ))
@@ -165,20 +169,12 @@
             pl.ds(d, product, stride=product), :
         ].astype(BF16)
 
-    for copy in later_loads:
-        copy.wait()
-    slots = index.shape[1]
-    counted = row_to_column(count[...].astype(F32), local)
-    lane = lax.broadcasted_iota(jnp.int32, (local, slots), 1)
-    live_index = jnp.where(lane.astype(F32) < counted, index[...], -1)
-    everyone_n = lax.broadcasted_iota(jnp.int32, (local, length), 1)
-    times = jnp.zeros((local, length), F32)
-    for t in range(slots):
-        times = times + jnp.where(live_index[:, t : t + 1] == everyone_n, 1.0, 0.0)
-
-    wait_bytes(right_all.at[pl.ds(0, n_row - 1)], recv_sem.at[5])
-    gathered = right_all.at[pl.ds(g * n_row, n_row)]
-    group(lambda q: send(gathered, gathered, 0, row, q))
+    def forward(r):
+        arrived = right_all.at[g * n_row + r]
+        wait_bytes(arrived, recv_sem.at[5 + r])
+        group(lambda q: send(arrived, arrived, 0, row, q))
+
+    rows_of_mesh(forward)
 
     wait_bytes(left_all.at[pl.ds(0, groups - 1)], recv_sem.at[1])
     left_rows = left_all[...].reshape(groups * slab, product).astype(BF16)
@@ -193,6 +189,17 @@
         for i in range(rows_own)
     ]
     t_joined = jnp.concatenate(t_pieces, 1).astype(BF16)
+
+    for copy in later_loads:
+        copy.wait()
+    slots = index.shape[1]
+    counted = row_to_column(count[...].astype(F32), local)
+    lane = lax.broadcasted_iota(jnp.int32, (local, slots), 1)
+    live_index = jnp.where(lane.astype(F32) < counted, index[...], -1)
+    everyone_n = lax.broadcasted_iota(jnp.int32, (local, length), 1)
+    times = jnp.zeros((local, length), F32)
+    for t in range(slots):
+        times = times + jnp.where(live_index[:, t : t + 1] == everyone_n, 1.0, 0.0)
 
     wait_bytes(node_all.at[pl.ds(0, groups - 1)], recv_sem.at[3])
     table = node_all[...].reshape(length, node_all.shape[2])
@@ -340,7 +347,7 @@
         pltpu.VMEM((groups, block, channels), BF16),
         pltpu.SemaphoreType.DMA((25,)),
         pltpu.SemaphoreType.DMA((6,)),
-        pltpu.SemaphoreType.DMA((6,)),
+        pltpu.SemaphoreType.DMA((5 + axes[1],)),
         pltpu.SemaphoreType.DMA((1,)),
     ]
     hbm = pl.BlockSpec(memory_space=pl.ANY)

time: 18.7 us -> 18.5 us (0.989)
  Pallas kernels: 17.9 us -> 17.7 us
    pallas_call x1, Pallas kernels: 17.3 us -> 17 us  [on_device(): pl.pallas_call(functools.partial(kernel, axes), out_shape=[pltpu.VMEM(pai...]
where the time goes in v3:
time: 18.5 us; the launch traced here: 18.3 us
  Pallas kernels  17.7 us (96%)
  between operations  0.65 us (4%)
    pallas_call x1, Pallas kernels, on_device(): pl.pallas_call(functools.partial(kernel, axes), out_shape=[pltpu.VMEM(pai...  17 us
    pallas_call x1, Pallas kernels, on_device(): pl.pallas_call(hand_over, out_shape=[jax.ShapeDtypeStruct(x.shape, x.dtyp...  0.65 us

profile of v3, /device:TPU:0, one launch (start us, length us, event | category | flops | bytes accessed | tf_op | source)
XLA Modules:
  0.0 18.3 jit_solution(15309358053295063314)
XLA Ops:
  0.6 17.0 %shard_map.265 = (bf16[8,16,128]{2,1,0:T(8,128)(2,1)S(1)}, bf16[8,64]{1,0:T(8,128)(2,1)S(1)}, f32[3,8]{1,0:T(4,128)S(1)}) custom-call(bf16[4,16,64]{2,1,0:T(8,128)(2,1)} %msa_hbm.1, s32[4,16]{1,0:T(4,128)} %ids_hbm.1, bf16[64,80]{1,0:T(8,128)(2,1)} %bitcast.13, f32[1,64]{1,0:T(1,128)} %bitcast.16, bf16[32,64]{1,0:T(8,128)(2,1)} %bitcast.14, ...), custom_call_target="tpu_custom_call" | custom-call | tf_op jit(solution)/shard_map/pallas_call | solution.py:354
  17.7 0.6 %shard_map.266 = (bf16[8,16,128]{2,1,0:T(8,128)(2,1)}, bf16[8,64]{1,0:T(8,128)(2,1)}, f32[3,8]{1,0:T(4,128)}) custom-call(bf16[8,16,128]{2,1,0:T(8,128)(2,1)S(1)} %get-tuple-element.9.refs_0_, bf16[8,64]{1,0:T(8,128)(2,1)S(1)} %get-tuple-element.10.refs_1_, f32[3,8]{1,0:T(4,128)S(1)} %get-tuple-element.11.refs_2_), custom_call_target="tpu_custom_call" | custom-call | tf_op jit(solution)/shard_map/pallas_call | solution.py:368
